TPU v7x, 32 devices: a whole 2x2x4 slice. The times are simulated.
32 devices in a mesh: dp: 16 (over z, y, x), stream: 2 (over core).
Axes of the slice: x: 2, y: 2, z: 4, core: 2. Of those that a mesh axis runs over, the one named last changes fastest.
Arguments:
- tokens: bfloat16 [16384, 512], P(('dp', 'stream')), may hold values from -6 to 6
- memory: bfloat16 [16384, 512], P(('dp', 'stream')), may hold values from -6 to 6
- cotangent: bfloat16 [16384, 512], P(('dp', 'stream')), may hold values from -6 to 6
- segments: int32 [16384], P(('dp', 'stream')), may hold values from 0 to 1039, as said below
- padding: int32 [16384], P(('dp', 'stream')), may hold values from 0 to 1, as said below
- priority: int32 [16384], P(('dp', 'stream')), may hold values from 0 to 4095
- threshold: int32 [16384], P(('dp', 'stream')), may hold values from 0 to 4096
- master: float32 [8192, 512], P(('dp', 'stream'))
- momentum: float32 [8192, 512], P(('dp', 'stream')), may hold values from -80 to 80
- vectors: float32 [8704], replicated
- vec_first: float32 [8704], replicated, may hold values from -224 to 224
- vec_second: float32 [8704], replicated, may hold values from 1.47456 to 5.89824
- step_count: int32 [1], replicated, may hold values from 2 to 20
Outputs:
- layer_out: bfloat16 [16384, 512], P(('dp', 'stream'))
- input_grad: float32 [16384, 512], P(('dp', 'stream'))
- memory_grad: float32 [16384, 512], P(('dp', 'stream'))
- new_momentum: float32 [8192, 512], P(('dp', 'stream'))
- new_master: float32 [8192, 512], P(('dp', 'stream'))
- new_vectors: float32 [8704], replicated
- new_vec_first: float32 [8704], replicated
- new_vec_second: float32 [8704], replicated
Inputs may be any that keep to these rules, and one draw needn't show every extreme that they name: `segments`: ids never fall and never cross an aligned block of 1024 rows. A block holds one whole document of 1024 tokens (some blocks in every draw) or sentences of 16 to 44 tokens, whose last one may be cut off by the block's end. `padding`: 1 exactly on the rows of a sentence cut off by its block's end.
All inputs are finite; a program needn't handle non-finite values.
Results may differ from a plain program's by a relative error of at most 0.025.
The roundings to bfloat16 on the way count: a program that leaves them out, or rounds other values in their place, can miss the bound.
Values may be sent and summed in bfloat16 or wider, within the bound.
A program may use at most 256 MiB of HBM per device.

v0:
```python
import jax
import jax.numpy as jnp
from jax import lax
from jax.sharding import PartitionSpec as P

D = 512
HEADS = 8
HEAD = 64
FF = 2048
NS_A = 3.4445
NS_B = -4.775
NS_C = 2.0315
MUON_RATE = 0.8
ADAM_RATE = 0.2
ADAM_DECAY = 0.01
HIGH = lax.Precision.HIGHEST


def partner(block, axis, stride):
    count = lax.axis_size(axis)
    route = []
    for low in range(count):
        high = low | 1 << stride
        if high != low and high < count:
            route += [(low, high), (high, low)]
    return lax.ppermute(block, axis, route)


def plain_dot(left_mat, right_mat):
    return jnp.dot(left_mat, right_mat, preferred_element_type=jnp.float32)


def lead_dot(left_mat, right_mat):
    return lax.dot_general(
        left_mat, right_mat, (((0,), (0,)), ((), ())), preferred_element_type=jnp.float32
    )


def last_dot(left_mat, right_mat):
    return lax.dot_general(
        left_mat, right_mat, (((1,), (1,)), ((), ())), preferred_element_type=jnp.float32
    )


def high_dot(left_mat, right_mat):
    return jnp.dot(left_mat, right_mat, precision=lax.Precision.HIGH)


def exact_lead(left_mat, right_mat):
    return lax.dot_general(left_mat, right_mat, (((0,), (0,)), ((), ())), precision=HIGH)


def split_rows(all_rows):
    attn_w = all_rows[: 8 * D].reshape(8, D, D)
    return (attn_w, all_rows[8 * D : 8 * D + FF], all_rows[8 * D + FF :])


def norm_forward(values, gain_vec, shift_vec):
    center = values - jnp.mean(values, axis=-1, keepdims=True)
    spread = lax.rsqrt(jnp.mean(center * center, axis=-1, keepdims=True) + 1e-05)
    normed = center * spread
    return (normed * gain_vec + shift_vec, normed, spread)


def norm_backward(normed, spread, gain_vec, grad_out):
    grad_gain = jnp.sum(grad_out * normed, axis=0)
    grad_shift = jnp.sum(grad_out, axis=0)
    scaled = grad_out * gain_vec
    grad_in = spread * (
        scaled
        - jnp.mean(scaled, axis=-1, keepdims=True)
        - normed * jnp.mean(scaled * normed, axis=-1, keepdims=True)
    )
    return (grad_in, grad_gain, grad_shift)


def split_heads(matrix):
    return matrix.reshape(matrix.shape[0], HEADS, HEAD)


def block_scores(queries, keys_all, visible):
    scores = jnp.einsum(
        "qhe,khe->hqk",
        split_heads(queries),
        split_heads(keys_all),
        preferred_element_type=jnp.float32,
    )
    return jnp.where(visible[None], scores * HEAD ** (-0.5), -1e30)


def attend_forward(queries, keys_all, values_all, visible):
    scores = block_scores(queries, keys_all, visible)
    row_max = jnp.max(scores, axis=-1, keepdims=True)
    expo = jnp.exp(scores - row_max)
    row_total = jnp.sum(expo, axis=-1, keepdims=True)
    weights_low = (expo / row_total).astype(jnp.bfloat16)
    mixed = jnp.einsum(
        "hqk,khe->qhe", weights_low, split_heads(values_all), preferred_element_type=jnp.float32
    )
    return (mixed.reshape(queries.shape[0], HEADS * HEAD), row_max + jnp.log(row_total))


def attend_backward(queries, keys_all, values_all, visible, logsum, grad_out):
    probs = jnp.exp(block_scores(queries, keys_all, visible) - logsum)
    grad_heads = split_heads(grad_out)
    grad_probs = jnp.einsum(
        "qhe,khe->hqk", grad_heads, split_heads(values_all), preferred_element_type=jnp.float32
    )
    inner_sum = jnp.sum(grad_probs * probs, axis=-1, keepdims=True)
    grad_scores = (probs * (grad_probs - inner_sum) * HEAD ** (-0.5)).astype(jnp.bfloat16)
    grad_q = jnp.einsum(
        "hqk,khe->qhe", grad_scores, split_heads(keys_all), preferred_element_type=jnp.float32
    )
    grad_k = jnp.einsum(
        "hqk,qhe->khe", grad_scores, split_heads(queries), preferred_element_type=jnp.float32
    )
    grad_v = jnp.einsum(
        "hqk,qhe->khe", probs.astype(jnp.bfloat16), grad_heads, preferred_element_type=jnp.float32
    )
    key_count = keys_all.shape[0]
    return (
        grad_q.reshape(queries.shape[0], HEADS * HEAD),
        grad_k.reshape(key_count, HEADS * HEAD),
        grad_v.reshape(key_count, HEADS * HEAD),
    )


def attend_all(queries, keys_all, values_all, visible):
    mixed, logsum = attend_forward(queries, keys_all, values_all, visible)
    logsums = [logsum]
    return (mixed, logsums)


def attend_back_all(queries, keys_all, values_all, visible, logsums, grad_out):
    block_rows = min(512, queries.shape[0])
    grad_q_parts = []
    grad_keys = jnp.zeros(keys_all.shape, jnp.float32)
    grad_values = jnp.zeros(values_all.shape, jnp.float32)
    for block_index, begin_row in enumerate(range(0, queries.shape[0], block_rows)):
        grad_q, grad_k, grad_v = attend_backward(
            queries, keys_all, values_all, visible, logsums[block_index], grad_out
        )
        grad_q_parts.append(grad_q)
        grad_keys = grad_k
        grad_values = grad_v
    return (grad_q_parts[0], grad_keys, grad_values)


def per_device(
    tokens,
    memory,
    cotangent,
    segments,
    padding,
    priority,
    threshold,
    master,
    momentum,
    vectors,
    vec_first,
    vec_second,
    step_count,
):

    def vector_part(position):
        return vectors[position * D : (position + 1) * D]

    low_master = master.astype(jnp.bfloat16)
    attn_w, w_in, w_out = split_rows(
        lax.all_gather(low_master, ("dp", "stream"), axis=0, tiled=True)
    )
    tokens_f32 = tokens.astype(jnp.float32)
    ln_one, normed_one, spread_one = norm_forward(tokens_f32, vector_part(0), vector_part(1))
    h_one = ln_one.astype(jnp.bfloat16)
    queries = (plain_dot(h_one, attn_w[0]) + vector_part(6)).astype(jnp.bfloat16)
    keys_own = plain_dot(h_one, attn_w[1]).astype(jnp.bfloat16)
    values_own = (plain_dot(h_one, attn_w[2]) + vector_part(7)).astype(jnp.bfloat16)
    mem_keys = plain_dot(memory, attn_w[5]).astype(jnp.bfloat16)
    mem_values = (plain_dot(memory, attn_w[6]) + vector_part(10)).astype(jnp.bfloat16)
    keys_all, values_all, mem_keys_all, mem_values_all = (
        lax.all_gather(keys_own, "stream", axis=0, tiled=True),
        lax.all_gather(values_own, "stream", axis=0, tiled=True),
        lax.all_gather(mem_keys, "stream", axis=0, tiled=True),
        lax.all_gather(mem_values, "stream", axis=0, tiled=True),
    )
    seg_all, pad_all, prio_all = (
        lax.all_gather(segments, "stream", axis=0, tiled=True),
        lax.all_gather(padding, "stream", axis=0, tiled=True),
        lax.all_gather(priority, "stream", axis=0, tiled=True),
    )
    own_rows = queries.shape[0]
    place = jnp.arange(own_rows, dtype=jnp.int32) + lax.axis_index("stream") * own_rows
    key_place = jnp.arange(seg_all.shape[0], dtype=jnp.int32)
    diagonal = place[:, None] == key_place[None, :]
    same_seg = segments[:, None] == seg_all[None, :]
    open_key = (pad_all == 0)[None, :]
    vis_self = same_seg & ((prio_all[None, :] < threshold[:, None]) & open_key | diagonal)
    vis_cross = same_seg & (open_key | diagonal)
    attn_out, lse_one = attend_all(queries, keys_all, values_all, vis_self)
    attn_low = attn_out.astype(jnp.bfloat16)
    res_one = tokens_f32 + plain_dot(attn_low, attn_w[3]) + vector_part(8)
    ln_two, normed_two, spread_two = norm_forward(res_one, vector_part(2), vector_part(3))
    h_two = ln_two.astype(jnp.bfloat16)
    cross_q = (plain_dot(h_two, attn_w[4]) + vector_part(9)).astype(jnp.bfloat16)
    cross_out, lse_two = attend_all(cross_q, mem_keys_all, mem_values_all, vis_cross)
    cross_low = cross_out.astype(jnp.bfloat16)
    res_two = res_one + plain_dot(cross_low, attn_w[7]) + vector_part(11)
    ln_three, normed_three, spread_three = norm_forward(res_two, vector_part(4), vector_part(5))
    h_three = ln_three.astype(jnp.bfloat16)
    pre_act = last_dot(h_three, w_in) + vectors[13 * D :]
    hidden = jnp.maximum(pre_act, 0.0).astype(jnp.bfloat16)
    layer_out = (res_two + plain_dot(hidden, w_out) + vector_part(12)).astype(jnp.bfloat16)
    grad_out_w = lead_dot(hidden, cotangent)
    grad_bias_out = jnp.sum(cotangent.astype(jnp.float32), axis=0)
    grad_hidden = last_dot(cotangent, w_out)
    grad_pre = jnp.where(pre_act > 0, grad_hidden, 0.0).astype(jnp.bfloat16)
    grad_bias_hidden = jnp.sum(grad_pre.astype(jnp.float32), axis=0)
    grad_in_w = lead_dot(grad_pre, h_three)
    grad_ln_three, grad_gain_three, grad_shift_three = norm_backward(
        normed_three, spread_three, vector_part(4), plain_dot(grad_pre, w_in)
    )
    grad_res_two = cotangent.astype(jnp.float32) + grad_ln_three
    grad_res_two_low = grad_res_two.astype(jnp.bfloat16)
    grad_bias_cross_o = jnp.sum(grad_res_two, axis=0)
    grad_cross_o_w = lead_dot(cross_low, grad_res_two_low)
    grad_cross = last_dot(grad_res_two_low, attn_w[7]).astype(jnp.bfloat16)
    grad_cq, grad_mk_all, grad_mv_all = attend_back_all(
        cross_q, mem_keys_all, mem_values_all, vis_cross, lse_two, grad_cross
    )
    grad_cq_low = grad_cq.astype(jnp.bfloat16)
    grad_bias_cq = jnp.sum(grad_cq_low.astype(jnp.float32), axis=0)
    grad_cq_w = lead_dot(h_two, grad_cq_low)
    grad_ln_two, grad_gain_two, grad_shift_two = norm_backward(
        normed_two, spread_two, vector_part(2), last_dot(grad_cq_low, attn_w[4])
    )
    grad_res_one = grad_res_two + grad_ln_two
    grad_res_one_low = grad_res_one.astype(jnp.bfloat16)
    grad_bias_o = jnp.sum(grad_res_one, axis=0)
    grad_o_w = lead_dot(attn_low, grad_res_one_low)
    grad_attn = last_dot(grad_res_one_low, attn_w[3]).astype(jnp.bfloat16)
    grad_q, grad_k_all, grad_v_all = attend_back_all(
        queries, keys_all, values_all, vis_self, lse_one, grad_attn
    )
    grad_k, grad_v, grad_mk, grad_mv = (
        lax.psum_scatter(grad_k_all, "stream", scatter_dimension=0, tiled=True),
        lax.psum_scatter(grad_v_all, "stream", scatter_dimension=0, tiled=True),
        lax.psum_scatter(grad_mk_all, "stream", scatter_dimension=0, tiled=True),
        lax.psum_scatter(grad_mv_all, "stream", scatter_dimension=0, tiled=True),
    )
    grad_q_low = grad_q.astype(jnp.bfloat16)
    grad_k_low = grad_k.astype(jnp.bfloat16)
    grad_v_low = grad_v.astype(jnp.bfloat16)
    grad_mk_low = grad_mk.astype(jnp.bfloat16)
    grad_mv_low = grad_mv.astype(jnp.bfloat16)
    grad_h_one = (
        last_dot(grad_q_low, attn_w[0])
        + last_dot(grad_k_low, attn_w[1])
        + last_dot(grad_v_low, attn_w[2])
    )
    grad_ln_one, grad_gain_one, grad_shift_one = norm_backward(
        normed_one, spread_one, vector_part(0), grad_h_one
    )
    input_grad = grad_res_one + grad_ln_one
    memory_grad = last_dot(grad_mk_low, attn_w[5]) + last_dot(grad_mv_low, attn_w[6])
    stacked = jnp.concatenate(
        [
            lead_dot(h_one, grad_q_low),
            lead_dot(h_one, grad_k_low),
            lead_dot(h_one, grad_v_low),
            grad_o_w,
            grad_cq_w,
            lead_dot(memory, grad_mk_low),
            lead_dot(memory, grad_mv_low),
            grad_cross_o_w,
            grad_in_w,
            grad_out_w,
        ],
        axis=0,
    )
    vec_local = jnp.concatenate(
        [
            grad_gain_one,
            grad_shift_one,
            grad_gain_two,
            grad_shift_two,
            grad_gain_three,
            grad_shift_three,
            jnp.sum(grad_q_low.astype(jnp.float32), axis=0),
            jnp.sum(grad_v_low.astype(jnp.float32), axis=0),
            grad_bias_o,
            grad_bias_cq,
            jnp.sum(grad_mv_low.astype(jnp.float32), axis=0),
            grad_bias_cross_o,
            grad_bias_out,
            grad_bias_hidden,
        ],
        axis=0,
    )
    grad_rows = lax.psum_scatter(stacked, ("dp", "stream"), scatter_dimension=0, tiled=True)
    grad_vec = lax.psum(vec_local, ("dp", "stream"))
    opt_rows = master.shape[0]
    device_index = lax.axis_index(("dp", "stream"))
    start_row = device_index * opt_rows
    in_ffn = start_row >= 8 * D
    att_bits = (D // opt_rows).bit_length() - 1
    ffn_bits = (FF // opt_rows).bit_length() - 1
    own_bits = jnp.where(in_ffn, ffn_bits, att_bits)
    new_momentum = 0.5 * momentum + grad_rows

    def gram_total(partial_value):
        for bit_pos in range(ffn_bits):
            other = partner(partial_value, ("dp", "stream"), bit_pos)
            partial_value = partial_value + jnp.where(bit_pos < own_bits, other, 0.0)
        return partial_value

    gram_first = gram_total(exact_lead(new_momentum, new_momentum))
    divisor = jnp.sqrt(jnp.trace(gram_first)) + 1e-07
    gram = gram_first / (divisor * divisor)
    unit = jnp.eye(D, dtype=jnp.float32)
    chain = None
    for turn in range(5):
        poly = NS_A * unit + NS_B * gram + NS_C * high_dot(gram, gram)
        chain = poly if chain is None else high_dot(chain, poly)
        if turn < 4:
            gram = high_dot(high_dot(gram, poly), poly)
    current = high_dot(new_momentum / divisor, chain)
    rate = MUON_RATE * jnp.where(in_ffn, (FF / D) ** 0.5, 1.0)
    new_master = master - rate * current
    count = step_count[0].astype(jnp.float32)
    new_first = 0.5 * vec_first + 0.5 * grad_vec
    new_second = 0.999 * vec_second + 0.001 * grad_vec * grad_vec
    first_fix = new_first / (1.0 - jnp.power(0.5, count))
    second_fix = new_second / (1.0 - jnp.power(0.999, count))
    new_vectors = vectors - ADAM_RATE * (
        first_fix / (jnp.sqrt(second_fix) + 1e-08) + ADAM_DECAY * vectors
    )
    return (
        layer_out,
        input_grad,
        memory_grad,
        new_momentum,
        new_master,
        new_vectors,
        new_first,
        new_second,
    )


def solution(mesh):
    return jax.shard_map(
        per_device,
        mesh=mesh,
        in_specs=(
            P(("dp", "stream"), None),
            P(("dp", "stream"), None),
            P(("dp", "stream"), None),
            P(("dp", "stream")),
            P(("dp", "stream")),
            P(("dp", "stream")),
            P(("dp", "stream")),
            P(("dp", "stream"), None),
            P(("dp", "stream"), None),
            P(),
            P(),
            P(),
            P(),
        ),
        out_specs=(
            P(("dp", "stream"), None),
            P(("dp", "stream"), None),
            P(("dp", "stream"), None),
            P(("dp", "stream"), None),
            P(("dp", "stream"), None),
            P(),
            P(),
            P(),
        ),
        check_vma=False,
    )
```

profile of v0, /device:TPU:0, one launch (start us, length us, event | category | flops | bytes accessed | tf_op | source)
XLA Modules:
  0.0 707.6 jit_solution(17345366208032327094)
XLA Ops:
  12.1 79.5 %all-gather.9.cloned.1.call-done = bf16[8192,512]{1,0:T(8,128)(2,1)} async-done(((bf16[256,512]{1,0:T(8,128)(2,1)}), bf16[8192,512]{1,0:T(8,128)(2,1)}) %all-gather.9.cloned.1.call-update) | async-done | bytes 8388624 | tf_op jit(solution)/shard_map/all_gather | solution.py:170
  107.7 2.9 compare_and_fusion
  116.7 3.2 fusion.153
  119.9 6.1 copy-done.1
  126.0 3.7 fusion.8
  131.2 8.2 %fusion.81 = bf16[8,64,512]{2,1,0:T(8,128)(2,1)S(1)} fusion(bf16[1024,8,64]{0,2,1:T(8,128)(2,1)S(1)} %bitcast.115, f32[8,512,1024]{2,1,0:T(8,128)} %copy-done.1, f32[8,512]{1,0:T(8,128)S(1)} %fusion.8, f32[8,512]{1,0:T(8,128)S(1)} %get-tuple-element.67), kind=kOutput, calls=%fused_computation.108 | convolution fusion | flops 549715968 | bytes 18382848 | tf_op jit(solution)/shard_map/hqk,khe->qhe/dot_general | solution.py:97
  145.0 4.5 fusion.155
  149.5 5.7 copy-done.2
  155.2 3.7 fusion.9
  160.5 8.0 %fusion.80 = bf16[8,64,512]{2,1,0:T(8,128)(2,1)S(1)} fusion(bf16[1024,8,64]{0,2,1:T(8,128)(2,1)S(1)} %bitcast.117, f32[8,512,1024]{2,1,0:T(8,128)} %copy-done.2, f32[8,512]{1,0:T(8,128)S(1)} %fusion.9, f32[8,512]{1,0:T(8,128)S(1)} %get-tuple-element.71), kind=kOutput, calls=%fused_computation.107 | convolution fusion | flops 549715968 | bytes 18382848 | tf_op jit(solution)/shard_map/hqk,khe->qhe/dot_general | solution.py:97
  170.4 3.1 fusion.51
  175.5 2.9 convert_reduce_fusion
  179.8 3.8 fusion.158
  193.0 9.3 %fusion.163 = f32[8,512,1024]{2,1,0:T(8,128)} fusion(bf16[512,8,64]{0,2,1:T(8,128)(2,1)S(1)} %bitcast.119, bf16[1024,8,64]{0,2,1:T(8,128)(2,1)} %bitcast.118), kind=kOutput, calls=%fused_computation.238 | convolution fusion | flops 536870912 | bytes 18350080 | tf_op jit(solution)/shard_map/qhe,khe->hqk/dot_general | solution.py:106
  202.3 30.8 %convert_reduce_fusion.4 = (f32[8,64]{1,0:T(8,128)S(1)}, bf16[8,64,512]{2,1,0:T(8,128)(2,1)}) fusion(bf16[1024,8,64]{0,2,1:T(8,128)(2,1)} %bitcast.126, f32[8,512,1024]{2,1,0:T(8,128)} %fusion.163, f32[8,512,1024]{2,1,0:T(8,128)} %copy-done.2, f32[8,512]{1,0:T(8,128)S(1)} %log_add_fusion.1), kind=kOutput, calls=%fused_computation.127 | convolution fusion | flops 567022080 | bytes 35145728 | tf_op jit(solution)/shard_map/hqk,khe->qhe/dot_general | solution.py:111
  245.2 9.3 %fusion.164 = f32[8,512,1024]{2,1,0:T(8,128)} fusion(bf16[512,8,64]{0,2,1:T(8,128)(2,1)S(1)} %bitcast.121, bf16[1024,8,64]{0,2,1:T(8,128)(2,1)} %bitcast.116), kind=kOutput, calls=%fused_computation.239 | convolution fusion | flops 536870912 | bytes 18350080 | tf_op jit(solution)/shard_map/qhe,khe->hqk/dot_general | solution.py:106
  254.5 30.9 %fusion.19 = f32[8,64,1024]{2,1,0:T(8,128)} fusion(bf16[512,8,64]{0,2,1:T(8,128)(2,1)} %bitcast.136, f32[8,512,1024]{2,1,0:T(8,128)} %fusion.164, f32[8,512,1024]{2,1,0:T(8,128)} %copy-done.1, f32[8,512]{1,0:T(8,128)S(1)} %log_add_fusion), kind=kOutput, calls=%fused_computation.22 | convolution fusion | flops 566236160 | bytes 36192256 | tf_op jit(solution)/shard_map/hqk,qhe->khe/dot_general | solution.py:114
  285.5 10.7 %fusion.24 = f32[8,64,1024]{2,1,0:T(8,128)} fusion(bf16[512,8,64]{0,2,1:T(8,128)(2,1)} %bitcast.122, f32[8,512,1024]{2,1,0:T(8,128)} %copy-done.1, f32[8,512]{1,0:T(8,128)S(1)} %log_add_fusion), kind=kOutput, calls=%fused_computation.24 | convolution fusion | flops 545259520 | bytes 19415040 | tf_op jit(solution)/shard_map/hqk,qhe->khe/dot_general | solution.py:117
  296.3 30.9 %fusion.13 = f32[8,64,1024]{2,1,0:T(8,128)} fusion(bf16[512,8,64]{0,2,1:T(8,128)(2,1)} %bitcast.138, f32[8,512,1024]{2,1,0:T(8,128)} %fusion.163, f32[8,512,1024]{2,1,0:T(8,128)} %copy-done.2, f32[8,512]{1,0:T(8,128)S(1)} %log_add_fusion.1), kind=kOutput, calls=%fused_computation.20 | convolution fusion | flops 566236160 | bytes 36192256 | tf_op jit(solution)/shard_map/hqk,qhe->khe/dot_general | solution.py:114
  327.3 10.7 %fusion.26 = f32[8,64,1024]{2,1,0:T(8,128)} fusion(bf16[512,8,64]{0,2,1:T(8,128)(2,1)} %bitcast.120, f32[8,512,1024]{2,1,0:T(8,128)} %copy-done.2, f32[8,512]{1,0:T(8,128)S(1)} %log_add_fusion.1), kind=kOutput, calls=%fused_computation.25 | convolution fusion | flops 545259520 | bytes 19415040 | tf_op jit(solution)/shard_map/hqk,qhe->khe/dot_general | solution.py:117
  338.1 30.6 %convert_reduce_fusion.6 = (f32[8,64]{1,0:T(8,128)S(1)}, bf16[8,64,512]{2,1,0:T(8,128)(2,1)}) fusion(bf16[1024,8,64]{0,2,1:T(8,128)(2,1)} %bitcast.124, f32[8,512,1024]{2,1,0:T(8,128)} %fusion.164, f32[8,512,1024]{2,1,0:T(8,128)} %copy-done.1, f32[8,512]{1,0:T(8,128)S(1)} %log_add_fusion), kind=kOutput, calls=%fused_computation.129 | convolution fusion | flops 567022080 | bytes 35145728 | tf_op jit(solution)/shard_map/hqk,khe->qhe/dot_general | solution.py:111
  371.2 2.8 convolution_dynamic-update-slice_fusion.6
  376.7 2.8 convolution_dynamic-update-slice_fusion.4
  382.1 2.8 fusion.58
  387.6 2.8 convolution_dynamic-update-slice_fusion.2
  390.4 5.0 convolution_dynamic-update-slice_fusion.1
  395.4 5.5 convolution_dynamic-update-slice_fusion
  401.8 5.0 fusion.67
  412.5 3.1 fusion.95
  415.6 166.6 %reduce-scatter.14.cloned.1.call-done = f32[256,512]{1,0:T(8,128)} async-done(((f32[8192,512]{1,0:T(8,128)}), f32[256,512]{1,0:T(8,128)}) %reduce-scatter.14.cloned.1.call-update) | async-done | bytes 524304 | tf_op jit(solution)/shard_map/reduce_scatter | solution.py:299
  595.7 59.5 %psum.7 = f32[8704]{0:T(1024)S(1)} all-reduce(f32[8704]{0:T(1024)S(1)} %constant_dynamic-update-slice_fusion.10), channel_id=1, replica_groups=mesh['dp'=16,'stream'=2] {'dp','stream'}, use_global_device_ids=true, to_apply=%region_38.39 | all-reduce | flops 8704 | bytes 69632 | tf_op jit(solution)/shard_map/psum | solution.py:300
  662.8 16.8 %collective-permute-done.2 = f32[512,512]{1,0:T(8,128)S(1)} collective-permute-done((f32[512,512]{1,0:T(8,128)S(1)}, f32[512,512]{1,0:T(8,128)S(1)}, u32[]{:S(2)}, u32[]{:S(2)}) %collective-permute-start.2) | collective-permute-done | bytes 1048608 | tf_op jit(solution)/shard_map/ppermute | solution.py:26
  (190 shorter events, 119.6 us)
Async XLA Ops:
  7.2 89.6 %copy-start = (bf16[512,512]{1,0:T(8,128)(2,1)S(1)}, bf16[512,512]{1,0:T(8,128)(2,1)}, u32[]{:S(2)}) copy-start(bf16[512,512]{1,0:T(8,128)(2,1)} %param.14) | copy-start | bytes 1572868
  7.2 84.5 %all-gather.9.cloned.1.call-start = ((), (), s32[]{:S(2)}) async-start(), calls=%async_computation.5 | async-start | bytes 8650752 | tf_op jit(solution)/shard_map/all_gather | solution.py:170
  9.1 105.5 %all-gather.13.cloned.1.call-start = ((), (), s32[]{:S(2)}) async-start(), calls=%async_computation.7 | async-start | bytes 1572864 | tf_op jit(solution)/shard_map/all_gather | solution.py:181
  94.2 35.6 %all-gather.11.cloned.1.call-start = ((), (), s32[]{:S(2)}) async-start(), calls=%async_computation.6 | async-start | bytes 1572864 | tf_op jit(solution)/shard_map/all_gather | solution.py:182
  96.7 44.7 %all-gather.17.cloned.1.call-start = ((), (), s32[]{:S(2)}) async-start(), calls=%async_computation.9 | async-start | bytes 1572864 | tf_op jit(solution)/shard_map/all_gather | solution.py:183
  99.1 59.9 %all-gather.15.cloned.1.call-start = ((), (), s32[]{:S(2)}) async-start(), calls=%async_computation.8 | async-start | bytes 1572864 | tf_op jit(solution)/shard_map/all_gather | solution.py:184
  112.9 258.3 %reduce-scatter.6.cloned.1.call-start = ((), (), s32[]{:S(2)}) async-start(), calls=%async_computation.10 | async-start | bytes 3145728 | tf_op jit(solution)/shard_map/reduce_scatter | solution.py:245
  114.6 15.1 %copy-start.22 = (bf16[512,512]{0,1:T(8,128)(2,1)}, bf16[512,512]{0,1:T(8,128)(2,1)S(1)}, u32[]{:S(2)}) copy-start(bf16[512,512]{0,1:T(8,128)(2,1)S(1)} %fusion.77) | copy-start | bytes 1572868
  116.6 13.0 %copy-start.14 = (bf16[1024,512]{0,1:T(8,128)(2,1)}, bf16[1024,512]{0,1:T(8,128)(2,1)S(1)}, u32[]{:S(2)}) copy-start(bf16[1024,512]{0,1:T(8,128)(2,1)S(1)} %copy.61) | copy-start | bytes 3145732
  119.9 6.1 copy-start.1
  131.2 8.2 %copy-start.10 = (bf16[1024,512]{0,1:T(8,128)(2,1)}, bf16[1024,512]{0,1:T(8,128)(2,1)S(1)}, u32[]{:S(2)}) copy-start(bf16[1024,512]{0,1:T(8,128)(2,1)S(1)} %copy.60) | copy-start | bytes 3145732
  142.9 15.9 %copy-start.15 = (bf16[1024,512]{0,1:T(8,128)(2,1)}, bf16[1024,512]{0,1:T(8,128)(2,1)S(1)}, u32[]{:S(2)}) copy-start(bf16[1024,512]{0,1:T(8,128)(2,1)S(1)} %copy.63) | copy-start | bytes 3145732
  145.0 13.9 %copy-start.23 = (bf16[512,512]{0,1:T(8,128)(2,1)}, bf16[512,512]{0,1:T(8,128)(2,1)S(1)}, u32[]{:S(2)}) copy-start(bf16[512,512]{0,1:T(8,128)(2,1)S(1)} %fusion.79) | copy-start | bytes 1572868
  160.5 8.0 %copy-start.11 = (bf16[1024,512]{0,1:T(8,128)(2,1)}, bf16[1024,512]{0,1:T(8,128)(2,1)S(1)}, u32[]{:S(2)}) copy-start(bf16[1024,512]{0,1:T(8,128)(2,1)S(1)} %copy.62) | copy-start | bytes 3145732
  160.5 15.1 %copy-start.17 = (bf16[512,512]{1,0:T(8,128)(2,1)S(1)}, bf16[512,512]{1,0:T(8,128)(2,1)}, u32[]{:S(2)}) copy-start(bf16[512,512]{1,0:T(8,128)(2,1)} %param.15) | copy-start | bytes 1572868
  168.5 15.2 %copy-start.20 = (bf16[8,64,512]{2,1,0:T(8,128)(2,1)}, bf16[8,64,512]{2,1,0:T(8,128)(2,1)S(1)}, u32[]{:S(2)}) copy-start(bf16[8,64,512]{2,1,0:T(8,128)(2,1)S(1)} %fusion.80) | copy-start | bytes 1572868
  285.5 88.5 %reduce-scatter.8.cloned.1.call-start = ((), (), s32[]{:S(2)}) async-start(), calls=%async_computation.11 | async-start | bytes 3145728 | tf_op jit(solution)/shard_map/reduce_scatter | solution.py:246
  296.3 85.8 %reduce-scatter.10.cloned.1.call-start = ((), (), s32[]{:S(2)}) async-start(), calls=%async_computation.12 | async-start | bytes 3145728 | tf_op jit(solution)/shard_map/reduce_scatter | solution.py:247
  327.2 57.6 %reduce-scatter.12.cloned.1.call-start = ((), (), s32[]{:S(2)}) async-start(), calls=%async_computation.13 | async-start | bytes 3145728 | tf_op jit(solution)/shard_map/reduce_scatter | solution.py:248
  338.0 244.1 %reduce-scatter.14.cloned.1.call-start = ((), (), s32[]{:S(2)}) async-start(), calls=%async_computation.14 | async-start | bytes 17301504 | tf_op jit(solution)/shard_map/reduce_scatter | solution.py:299
  382.0 13.4 %copy-start.18 = (bf16[512,512]{1,0:T(8,128)(2,1)S(1)}, bf16[512,512]{1,0:T(8,128)(2,1)}, u32[]{:S(2)}) copy-start(bf16[512,512]{1,0:T(8,128)(2,1)} %param.15) | copy-start | bytes 1572868
  395.4 6.3 copy-start.27
  400.9 185.6 %copy-start.4 = (f32[512,512]{0,1:T(8,128)S(1)}, f32[512,512]{0,1:T(8,128)}, u32[]{:S(2)}) copy-start(f32[512,512]{0,1:T(8,128)} %copy-done.3) | copy-start | bytes 3145732
  406.7 188.8 %copy-start.7 = (f32[512,512]{0,1:T(8,128)S(1)}, f32[512,512]{0,1:T(8,128)}, u32[]{:S(2)}) copy-start(f32[512,512]{0,1:T(8,128)} %reduce-scatter.12.cloned.1.call-done) | copy-start | bytes 3145732
  409.0 253.1 %copy-start.24 = (f32[8704]{0:T(1024)S(1)}, f32[8704]{0:T(1024)}, u32[]{:S(2)}) copy-start(f32[8704]{0:T(1024)} %param.22) | copy-start | bytes 104452
  409.0 253.1 %copy-start.25 = (f32[8704]{0:T(1024)S(1)}, f32[8704]{0:T(1024)}, u32[]{:S(2)}) copy-start(f32[8704]{0:T(1024)} %param.24) | copy-start | bytes 104452
  409.0 253.1 %copy-start.26 = (f32[8704]{0:T(1024)S(1)}, f32[8704]{0:T(1024)}, u32[]{:S(2)}) copy-start(f32[8704]{0:T(1024)} %param.23) | copy-start | bytes 104452
  586.2 6.8 collective-permute-start
  594.8 60.4 %collective-permute-start.1 = (f32[512,512]{1,0:T(8,128)S(1)}, f32[512,512]{1,0:T(8,128)}, u32[]{:S(2)}, u32[]{:S(2)}) collective-permute-start(f32[512,512]{1,0:T(8,128)S(1)} %select_add_fusion.7), channel_id=1, source_target_pairs={{0,2},{2,0},{1,3},{3,1},{4,6},{6,4},{5,7},{7,5},{8,10},{10,8},{9,1... | collective-permute-start | bytes 3145736 | tf_op jit(solution)/shard_map/ppermute | solution.py:26
  655.5 24.2 %collective-permute-start.2 = (f32[512,512]{1,0:T(8,128)S(1)}, f32[512,512]{1,0:T(8,128)S(1)}, u32[]{:S(2)}, u32[]{:S(2)}) collective-permute-start(f32[512,512]{1,0:T(8,128)S(1)} %select_add_fusion.6), channel_id=1, source_target_pairs={{0,4},{4,0},{1,5},{5,1},{2,6},{6,2},{3,7},{7,3},{8,12},{12,8},{9,1... | collective-permute-start | bytes 3145736 | tf_op jit(solution)/shard_map/ppermute | solution.py:26
  687.4 11.6 %copy-start.9 = (f32[256,512]{1,0:T(8,128)S(1)}, f32[256,512]{1,0:T(8,128)}, u32[]{:S(2)}) copy-start(f32[256,512]{1,0:T(8,128)} %copy-done.8) | copy-start | bytes 1572868
  687.4 11.6 %copy-start.19 = (f32[256,512]{1,0:T(8,128)S(1)}, f32[256,512]{1,0:T(8,128)}, u32[]{:S(2)}) copy-start(f32[256,512]{1,0:T(8,128)} %param.20) | copy-start | bytes 1572868
  (9 other events, 15.4 us)
Sparse Core Ops, SparseCore 0:
  11.4 80.1 all-gather.8
  94.3 7.6 all-gather.12
  104.1 10.1 all-gather.10
  116.3 10.1 all-gather.16
  128.5 10.1 all-gather.14
  285.6 8.0 reduce-scatter.5
  296.4 10.3 reduce-scatter.7
  327.3 7.8 reduce-scatter.9
  338.1 10.2 reduce-scatter.11
  401.0 181.0 reduce-scatter.13
where the time goes:
time: 713 us; the launch traced here: 708 us
  matrix products  289 us (41%)
  waiting for transfers between devices  263 us (37%)
  blocking collectives  65.2 us (9%)
  local copies, waits for them, and re-layouts  40 us (6%)
  other arithmetic  30.2 us (4%)
  between operations  16.8 us (2%)
    reduce_scatter x1, waiting for transfers between devices, per_device(): lax.psum_scatter(stacked, ('dp', 'stream'), scatter_dimension=0, tiled=True)  167 us
    all_gather x1, waiting for transfers between devices, per_device(): lax.all_gather(low_master, ('dp', 'stream'), axis=0, tiled=True)  79.5 us
    dot_general x2, matrix products, attend_backward(): jnp.einsum('hqk,qhe->khe', grad_scores, split_heads(queries), preferred_e...  61.8 us
    dot_general x2, matrix products, attend_backward(): jnp.einsum('hqk,khe->qhe', grad_scores, split_heads(keys_all), preferred_...  61.4 us
    psum x1, blocking collectives, per_device(): grad_vec = lax.psum(vec_local, ('dp', 'stream'))  59.5 us
    dot_general x10, matrix products, lead_dot(): lax.dot_general(left_mat, right_mat, (((0,), (0,)), ((), ())), preferred_...  32.2 us
    unnamed x73, local copies, waits for them, and re-layouts  27.6 us
    dot_general x10, matrix products, plain_dot(): return jnp.dot(left_mat, right_mat, preferred_element_type=jnp.float32)  25.5 us
  transfers between devices with their start and end apart: 13, of which 3 were waited for; matrix products, arithmetic and copies ran while one was open for 25% of the time, Pallas kernels for 0%

commit v1 on v0

--- a/solution.py
+++ b/solution.py
@@ -297,7 +297,7 @@
         axis=0,
     )
     grad_rows = lax.psum_scatter(stacked, ("dp", "stream"), scatter_dimension=0, tiled=True)
-    grad_vec = lax.psum(vec_local, ("dp", "stream"))
+    grad_vec = jnp.sum(lax.all_gather(vec_local, axis_name=("dp", "stream")), 0)
     opt_rows = master.shape[0]
     device_index = lax.axis_index(("dp", "stream"))
     start_row = device_index * opt_rows

time: 713 us -> 687 us (0.964)
  blocking collectives: 65.2 us -> 5.72 us
  waiting for transfers between devices: 263 us -> 288 us
    psum x1 -> x0, blocking collectives: 59.5 us -> none  [per_device(): grad_vec = lax.psum(vec_local, ('dp', 'stream'))]
    all_gather x0 -> x1, waiting for transfers between devices: none -> 19.6 us  [per_device(): grad_vec = jnp.sum(lax.all_gather(vec_local, axis_name=('dp', 'stream')), 0)]
    unnamed x73 -> x72, local copies, waits for them, and re-layouts: 27.6 us -> 26.9 us
  transfers between devices with their start and end apart: 13 -> 14, of which waited for: 3 -> 5; matrix products, arithmetic and copies ran while one was open for 25% -> 26% of each run, Pallas kernels for 0% -> 0%
where the time goes in v1:
time: 687 us; the launch traced here: 681 us
  matrix products  292 us (43%)
  waiting for transfers between devices  288 us (42%)
  local copies, waits for them, and re-layouts  39.3 us (6%)
  other arithmetic  35.5 us (5%)
  between operations  16.4 us (2%)
    reduce_scatter x1, waiting for transfers between devices, per_device(): lax.psum_scatter(stacked, ('dp', 'stream'), scatter_dimension=0, tiled=True)  172 us
    all_gather x1, waiting for transfers between devices, per_device(): lax.all_gather(low_master, ('dp', 'stream'), axis=0, tiled=True)  79.5 us
    dot_general x2, matrix products, attend_backward(): jnp.einsum('hqk,qhe->khe', grad_scores, split_heads(queries), preferred_e...  61.8 us
    dot_general x2, matrix products, attend_backward(): jnp.einsum('hqk,khe->qhe', grad_scores, split_heads(keys_all), preferred_...  61.1 us
    dot_general x10, matrix products, lead_dot(): lax.dot_general(left_mat, right_mat, (((0,), (0,)), ((), ())), preferred_...  32.2 us
    unnamed x72, local copies, waits for them, and re-layouts  26.9 us
    dot_general x10, matrix products, plain_dot(): return jnp.dot(left_mat, right_mat, preferred_element_type=jnp.float32)  25.5 us
    dot_general x10, matrix products, last_dot(): lax.dot_general(left_mat, right_mat, (((1,), (1,)), ((), ())), preferred_...  22.8 us
  transfers between devices with their start and end apart: 14, of which 5 were waited for; matrix products, arithmetic and copies ran while one was open for 26% of the time, Pallas kernels for 0%

profile of v1, /device:TPU:0, one launch (start us, length us, event | category | flops | bytes accessed | tf_op | source)
XLA Modules:
  0.0 680.8 jit_solution(5933075405458351776)
XLA Ops:
  12.1 79.5 %all-gather.12.cloned.1.call-done = bf16[8192,512]{1,0:T(8,128)(2,1)} async-done(((bf16[256,512]{1,0:T(8,128)(2,1)}), bf16[8192,512]{1,0:T(8,128)(2,1)}) %all-gather.12.cloned.1.call-update) | async-done | bytes 8388624 | tf_op jit(solution)/shard_map/all_gather | solution.py:170
  107.7 2.9 compare_and_fusion
  116.6 3.2 fusion.153
  119.8 6.1 copy-done.1
  125.9 3.7 fusion.8
  131.2 8.2 %fusion.81 = bf16[8,64,512]{2,1,0:T(8,128)(2,1)S(1)} fusion(bf16[1024,8,64]{0,2,1:T(8,128)(2,1)S(1)} %bitcast.115, f32[8,512,1024]{2,1,0:T(8,128)} %copy-done.1, f32[8,512]{1,0:T(8,128)S(1)} %fusion.8, f32[8,512]{1,0:T(8,128)S(1)} %get-tuple-element.67), kind=kOutput, calls=%fused_computation.108 | convolution fusion | flops 549715968 | bytes 18382848 | tf_op jit(solution)/shard_map/hqk,khe->qhe/dot_general | solution.py:97
  144.9 4.5 fusion.155
  149.4 5.7 copy-done.2
  155.1 3.7 fusion.9
  160.4 8.0 %fusion.80 = bf16[8,64,512]{2,1,0:T(8,128)(2,1)S(1)} fusion(bf16[1024,8,64]{0,2,1:T(8,128)(2,1)S(1)} %bitcast.117, f32[8,512,1024]{2,1,0:T(8,128)} %copy-done.2, f32[8,512]{1,0:T(8,128)S(1)} %fusion.9, f32[8,512]{1,0:T(8,128)S(1)} %get-tuple-element.71), kind=kOutput, calls=%fused_computation.107 | convolution fusion | flops 549715968 | bytes 18382848 | tf_op jit(solution)/shard_map/hqk,khe->qhe/dot_general | solution.py:97
  170.4 3.1 fusion.51
  175.4 2.9 convert_reduce_fusion
  179.8 3.8 fusion.158
  193.0 9.3 %fusion.163 = f32[8,512,1024]{2,1,0:T(8,128)} fusion(bf16[512,8,64]{0,2,1:T(8,128)(2,1)S(1)} %bitcast.119, bf16[1024,8,64]{0,2,1:T(8,128)(2,1)} %bitcast.118), kind=kOutput, calls=%fused_computation.238 | convolution fusion | flops 536870912 | bytes 18350080 | tf_op jit(solution)/shard_map/qhe,khe->hqk/dot_general | solution.py:106
  202.3 30.6 %convert_reduce_fusion.4 = (f32[8,64]{1,0:T(8,128)S(1)}, bf16[8,64,512]{2,1,0:T(8,128)(2,1)}) fusion(bf16[1024,8,64]{0,2,1:T(8,128)(2,1)} %bitcast.126, f32[8,512,1024]{2,1,0:T(8,128)} %fusion.163, f32[8,512,1024]{2,1,0:T(8,128)} %copy-done.2, f32[8,512]{1,0:T(8,128)S(1)} %log_add_fusion.1), kind=kOutput, calls=%fused_computation.127 | convolution fusion | flops 567022080 | bytes 35145728 | tf_op jit(solution)/shard_map/hqk,khe->qhe/dot_general | solution.py:111
  245.0 9.3 %fusion.164 = f32[8,512,1024]{2,1,0:T(8,128)} fusion(bf16[512,8,64]{0,2,1:T(8,128)(2,1)S(1)} %bitcast.121, bf16[1024,8,64]{0,2,1:T(8,128)(2,1)} %bitcast.116), kind=kOutput, calls=%fused_computation.239 | convolution fusion | flops 536870912 | bytes 18350080 | tf_op jit(solution)/shard_map/qhe,khe->hqk/dot_general | solution.py:106
  254.3 30.9 %fusion.19 = f32[8,64,1024]{2,1,0:T(8,128)} fusion(bf16[512,8,64]{0,2,1:T(8,128)(2,1)} %bitcast.136, f32[8,512,1024]{2,1,0:T(8,128)} %fusion.164, f32[8,512,1024]{2,1,0:T(8,128)} %copy-done.1, f32[8,512]{1,0:T(8,128)S(1)} %log_add_fusion), kind=kOutput, calls=%fused_computation.22 | convolution fusion | flops 566236160 | bytes 36192256 | tf_op jit(solution)/shard_map/hqk,qhe->khe/dot_general | solution.py:114
  285.2 10.7 %fusion.24 = f32[8,64,1024]{2,1,0:T(8,128)} fusion(bf16[512,8,64]{0,2,1:T(8,128)(2,1)} %bitcast.122, f32[8,512,1024]{2,1,0:T(8,128)} %copy-done.1, f32[8,512]{1,0:T(8,128)S(1)} %log_add_fusion), kind=kOutput, calls=%fused_computation.24 | convolution fusion | flops 545259520 | bytes 19415040 | tf_op jit(solution)/shard_map/hqk,qhe->khe/dot_general | solution.py:117
  296.0 30.9 %fusion.13 = f32[8,64,1024]{2,1,0:T(8,128)} fusion(bf16[512,8,64]{0,2,1:T(8,128)(2,1)} %bitcast.138, f32[8,512,1024]{2,1,0:T(8,128)} %fusion.163, f32[8,512,1024]{2,1,0:T(8,128)} %copy-done.2, f32[8,512]{1,0:T(8,128)S(1)} %log_add_fusion.1), kind=kOutput, calls=%fused_computation.20 | convolution fusion | flops 566236160 | bytes 36192256 | tf_op jit(solution)/shard_map/hqk,qhe->khe/dot_general | solution.py:114
  327.4 10.8 %fusion.26 = f32[8,64,1024]{2,1,0:T(8,128)} fusion(bf16[512,8,64]{0,2,1:T(8,128)(2,1)} %bitcast.120, f32[8,512,1024]{2,1,0:T(8,128)} %copy-done.2, f32[8,512]{1,0:T(8,128)S(1)} %log_add_fusion.1), kind=kOutput, calls=%fused_computation.25 | convolution fusion | flops 545259520 | bytes 19415040 | tf_op jit(solution)/shard_map/hqk,qhe->khe/dot_general | solution.py:117
  338.2 30.5 %convert_reduce_fusion.6 = (f32[8,64]{1,0:T(8,128)S(1)}, bf16[8,64,512]{2,1,0:T(8,128)(2,1)}) fusion(bf16[1024,8,64]{0,2,1:T(8,128)(2,1)} %bitcast.124, f32[8,512,1024]{2,1,0:T(8,128)} %fusion.164, f32[8,512,1024]{2,1,0:T(8,128)} %copy-done.1, f32[8,512]{1,0:T(8,128)S(1)} %log_add_fusion), kind=kOutput, calls=%fused_computation.129 | convolution fusion | flops 567022080 | bytes 35145728 | tf_op jit(solution)/shard_map/hqk,khe->qhe/dot_general | solution.py:111
  376.7 2.8 convolution_dynamic-update-slice_fusion.4
  387.5 2.8 convolution_dynamic-update-slice_fusion.2
  390.4 5.0 convolution_dynamic-update-slice_fusion.1
  395.4 5.4 convolution_dynamic-update-slice_fusion
  405.6 3.0 fusion.95
  410.1 172.1 %reduce-scatter.14.cloned.1.call-done = f32[256,512]{1,0:T(8,128)} async-done(((f32[8192,512]{1,0:T(8,128)}), f32[256,512]{1,0:T(8,128)}) %reduce-scatter.14.cloned.1.call-update) | async-done | bytes 524304 | tf_op jit(solution)/shard_map/reduce_scatter | solution.py:299
  592.8 5.0 fusion.67
  602.7 16.0 %collective-permute-done.1 = f32[512,512]{1,0:T(8,128)} collective-permute-done((f32[512,512]{1,0:T(8,128)}, f32[512,512]{1,0:T(8,128)}, u32[]{:S(2)}, u32[]{:S(2)}) %collective-permute-start.1) | collective-permute-done | bytes 1048608 | tf_op jit(solution)/shard_map/ppermute | solution.py:26
  624.0 2.8 convolution_add_fusion.2
  626.8 19.6 %all-gather.22.cloned.1.call-done = f32[32,1,8704]{2,1,0:T(1,128)} async-done(((f32[1,1,8704]{2,1,0:T(1,128)}), f32[32,1,8704]{2,1,0:T(1,128)}) %all-gather.22.cloned.1.call-update) | async-done | bytes 1114128 | tf_op jit(solution)/shard_map/all_gather | solution.py:300
  651.5 3.1 fusion.97
  (192 shorter events, 128.3 us)
Async XLA Ops:
  7.2 89.6 %copy-start = (bf16[512,512]{1,0:T(8,128)(2,1)S(1)}, bf16[512,512]{1,0:T(8,128)(2,1)}, u32[]{:S(2)}) copy-start(bf16[512,512]{1,0:T(8,128)(2,1)} %param.14) | copy-start | bytes 1572868
  7.2 84.5 %all-gather.12.cloned.1.call-start = ((), (), s32[]{:S(2)}) async-start(), calls=%async_computation.5 | async-start | bytes 8650752 | tf_op jit(solution)/shard_map/all_gather | solution.py:170
  9.1 105.5 %all-gather.16.cloned.1.call-start = ((), (), s32[]{:S(2)}) async-start(), calls=%async_computation.7 | async-start | bytes 1572864 | tf_op jit(solution)/shard_map/all_gather | solution.py:181
  94.2 35.5 %all-gather.14.cloned.1.call-start = ((), (), s32[]{:S(2)}) async-start(), calls=%async_computation.6 | async-start | bytes 1572864 | tf_op jit(solution)/shard_map/all_gather | solution.py:182
  96.7 44.6 %all-gather.20.cloned.1.call-start = ((), (), s32[]{:S(2)}) async-start(), calls=%async_computation.9 | async-start | bytes 1572864 | tf_op jit(solution)/shard_map/all_gather | solution.py:183
  99.1 59.8 %all-gather.18.cloned.1.call-start = ((), (), s32[]{:S(2)}) async-start(), calls=%async_computation.8 | async-start | bytes 1572864 | tf_op jit(solution)/shard_map/all_gather | solution.py:184
  112.9 258.3 %reduce-scatter.6.cloned.1.call-start = ((), (), s32[]{:S(2)}) async-start(), calls=%async_computation.10 | async-start | bytes 3145728 | tf_op jit(solution)/shard_map/reduce_scatter | solution.py:245
  114.6 15.0 %copy-start.21 = (bf16[512,512]{0,1:T(8,128)(2,1)}, bf16[512,512]{0,1:T(8,128)(2,1)S(1)}, u32[]{:S(2)}) copy-start(bf16[512,512]{0,1:T(8,128)(2,1)S(1)} %fusion.77) | copy-start | bytes 1572868
  116.6 13.0 %copy-start.13 = (bf16[1024,512]{0,1:T(8,128)(2,1)}, bf16[1024,512]{0,1:T(8,128)(2,1)S(1)}, u32[]{:S(2)}) copy-start(bf16[1024,512]{0,1:T(8,128)(2,1)S(1)} %copy.61) | copy-start | bytes 3145732
  119.8 6.1 copy-start.1
  131.2 8.2 %copy-start.9 = (bf16[1024,512]{0,1:T(8,128)(2,1)}, bf16[1024,512]{0,1:T(8,128)(2,1)S(1)}, u32[]{:S(2)}) copy-start(bf16[1024,512]{0,1:T(8,128)(2,1)S(1)} %copy.60) | copy-start | bytes 3145732
  142.9 15.9 %copy-start.14 = (bf16[1024,512]{0,1:T(8,128)(2,1)}, bf16[1024,512]{0,1:T(8,128)(2,1)S(1)}, u32[]{:S(2)}) copy-start(bf16[1024,512]{0,1:T(8,128)(2,1)S(1)} %copy.63) | copy-start | bytes 3145732
  144.9 13.9 %copy-start.22 = (bf16[512,512]{0,1:T(8,128)(2,1)}, bf16[512,512]{0,1:T(8,128)(2,1)S(1)}, u32[]{:S(2)}) copy-start(bf16[512,512]{0,1:T(8,128)(2,1)S(1)} %fusion.79) | copy-start | bytes 1572868
  160.4 8.0 %copy-start.10 = (bf16[1024,512]{0,1:T(8,128)(2,1)}, bf16[1024,512]{0,1:T(8,128)(2,1)S(1)}, u32[]{:S(2)}) copy-start(bf16[1024,512]{0,1:T(8,128)(2,1)S(1)} %copy.62) | copy-start | bytes 3145732
  160.4 15.0 %copy-start.16 = (bf16[512,512]{1,0:T(8,128)(2,1)S(1)}, bf16[512,512]{1,0:T(8,128)(2,1)}, u32[]{:S(2)}) copy-start(bf16[512,512]{1,0:T(8,128)(2,1)} %param.15) | copy-start | bytes 1572868
  168.4 15.2 %copy-start.19 = (bf16[8,64,512]{2,1,0:T(8,128)(2,1)}, bf16[8,64,512]{2,1,0:T(8,128)(2,1)S(1)}, u32[]{:S(2)}) copy-start(bf16[8,64,512]{2,1,0:T(8,128)(2,1)S(1)} %fusion.80) | copy-start | bytes 1572868
  285.2 88.8 %reduce-scatter.8.cloned.1.call-start = ((), (), s32[]{:S(2)}) async-start(), calls=%async_computation.11 | async-start | bytes 3145728 | tf_op jit(solution)/shard_map/reduce_scatter | solution.py:246
  296.0 86.1 %reduce-scatter.10.cloned.1.call-start = ((), (), s32[]{:S(2)}) async-start(), calls=%async_computation.12 | async-start | bytes 3145728 | tf_op jit(solution)/shard_map/reduce_scatter | solution.py:247
  326.9 57.9 %reduce-scatter.12.cloned.1.call-start = ((), (), s32[]{:S(2)}) async-start(), calls=%async_computation.13 | async-start | bytes 3145728 | tf_op jit(solution)/shard_map/reduce_scatter | solution.py:248
  338.2 244.0 %reduce-scatter.14.cloned.1.call-start = ((), (), s32[]{:S(2)}) async-start(), calls=%async_computation.14 | async-start | bytes 17301504 | tf_op jit(solution)/shard_map/reduce_scatter | solution.py:299
  382.0 13.4 %copy-start.17 = (bf16[512,512]{1,0:T(8,128)(2,1)S(1)}, bf16[512,512]{1,0:T(8,128)(2,1)}, u32[]{:S(2)}) copy-start(bf16[512,512]{1,0:T(8,128)(2,1)} %param.15) | copy-start | bytes 1572868
  400.9 192.0 %copy-start.26 = (f32[512]{0:T(512)S(1)}, f32[512]{0:T(512)}, u32[]{:S(2)}) copy-start(f32[512]{0:T(512)} %get-tuple-element.52) | copy-start | bytes 6148
  400.9 198.9 %copy-start.4 = (f32[512,512]{0,1:T(8,128)S(1)}, f32[512,512]{0,1:T(8,128)}, u32[]{:S(2)}) copy-start(f32[512,512]{0,1:T(8,128)} %copy-done.3) | copy-start | bytes 3145732
  400.9 245.5 %all-gather.22.cloned.1.call-start = ((), (), s32[]{:S(2)}) async-start(), calls=%async_computation.15 | async-start | bytes 1148928 | tf_op jit(solution)/shard_map/all_gather | solution.py:300
  584.3 64.0 %copy-start.23 = (f32[8704]{0:T(1024)S(1)}, f32[8704]{0:T(1024)}, u32[]{:S(2)}) copy-start(f32[8704]{0:T(1024)} %param.22) | copy-start | bytes 104452
  584.3 64.1 %copy-start.24 = (f32[8704]{0:T(1024)S(1)}, f32[8704]{0:T(1024)}, u32[]{:S(2)}) copy-start(f32[8704]{0:T(1024)} %param.24) | copy-start | bytes 104452
  584.3 64.1 %copy-start.25 = (f32[8704]{0:T(1024)S(1)}, f32[8704]{0:T(1024)}, u32[]{:S(2)}) copy-start(f32[8704]{0:T(1024)} %param.23) | copy-start | bytes 104452
  586.3 3.0 collective-permute-start
  592.0 26.7 %collective-permute-start.1 = (f32[512,512]{1,0:T(8,128)}, f32[512,512]{1,0:T(8,128)}, u32[]{:S(2)}, u32[]{:S(2)}) collective-permute-start(f32[512,512]{1,0:T(8,128)} %select_add_fusion.7), channel_id=1, source_target_pairs={{0,2},{2,0},{1,3},{3,1},{4,6},{6,4},{5,7},{7,5},{8,10},{10,8},{9,1... | collective-permute-start | bytes 3145736 | tf_op jit(solution)/shard_map/ppermute | solution.py:26
  620.1 28.9 %collective-permute-start.2 = (f32[512,512]{1,0:T(8,128)S(1)}, f32[512,512]{1,0:T(8,128)S(1)}, u32[]{:S(2)}, u32[]{:S(2)}) collective-permute-start(f32[512,512]{1,0:T(8,128)S(1)} %select_add_fusion.6), channel_id=1, source_target_pairs={{0,4},{4,0},{1,5},{5,1},{2,6},{6,2},{3,7},{7,3},{8,12},{12,8},{9,1... | collective-permute-start | bytes 3145736 | tf_op jit(solution)/shard_map/ppermute | solution.py:26
  661.3 11.3 %copy-start.8 = (f32[256,512]{1,0:T(8,128)S(1)}, f32[256,512]{1,0:T(8,128)}, u32[]{:S(2)}) copy-start(f32[256,512]{1,0:T(8,128)} %copy-done.7) | copy-start | bytes 1572868
  661.3 11.3 %copy-start.18 = (f32[256,512]{1,0:T(8,128)S(1)}, f32[256,512]{1,0:T(8,128)}, u32[]{:S(2)}) copy-start(f32[256,512]{1,0:T(8,128)} %param.20) | copy-start | bytes 1572868
  (9 other events, 15.4 us)
Sparse Core Ops, SparseCore 0:
  11.4 80.1 all-gather.11
  94.3 7.6 all-gather.15
  104.1 10.1 all-gather.13
  116.3 10.1 all-gather.19
  128.5 10.1 all-gather.17
  285.3 7.9 reduce-scatter.5
  296.1 10.4 reduce-scatter.7
  327.0 7.8 reduce-scatter.9
  338.3 9.7 reduce-scatter.11
  401.0 181.1 reduce-scatter.13
  588.7 57.6 all-gather.21
